TPU v7x, 32 devices: a whole 2x2x4 slice. The times are simulated.
32 devices in a mesh: pipe: 2 (over y), dp: 4 (over z), tensor: 4 (over x, core).
Axes of the slice: x: 2, y: 2, z: 4, core: 2. Of those that a mesh axis runs over, the one named last changes fastest.
Arguments:
- tokens: bfloat16 [3072, 8192], P(('pipe', 'dp'), 'tensor'), parts along dimension 0, may hold values from -6 to 6
- pattern: int32 [128, 6], P('pipe'), parts along dimension 0, may hold values from 0 to 31, as said below
- blocks: bfloat16 [128, 6, 256, 256], P(('pipe', 'tensor'), None, 'dp'), parts along dimension 0, may hold values from -0.15625 to 0.15625
- left_factor: bfloat16 [16384, 512], P(('pipe', 'tensor'), 'dp'), parts along dimension 0, may hold values from -0.0625 to 0.0625
- right_factor: bfloat16 [1024, 16384], P(('pipe', 'dp'), 'tensor'), parts along dimension 0, may hold values from -0.25 to 0.25
- cotangent: bfloat16 [3072, 16384], P(('pipe', 'dp'), 'tensor'), parts along dimension 0, may hold values from -6 to 6
Outputs:
- hidden: bfloat16 [3072, 16384], P(('pipe', 'dp'), 'tensor'), parts along dimension 0
- token_grad: float32 [3072, 8192], P(('pipe', 'dp'), 'tensor'), parts along dimension 0
- block_grad: float32 [128, 6, 256, 256], P(('pipe', 'tensor'), None, 'dp'), parts along dimension 0
- left_grad: float32 [16384, 512], P(('pipe', 'tensor'), 'dp'), parts along dimension 0
- right_grad: float32 [1024, 16384], P(('pipe', 'dp'), 'tensor'), parts along dimension 0
There are 2 independent parts, one for each index of `pipe`. A program takes and returns all parts, laid end to end along the dimension named above; each array names one. Nothing has to cross between parts.
Inputs may be any that keep to these rules, and one draw needn't show every extreme that they name: `pattern`: row j lists the 6 input blocks feeding hidden block j: under a relabeling of the 32 input blocks drawn from the seed, they are the labels of (j mod 32) XOR s for s = 0 and then the powers of two below 32 in rising order; a row's entries are distinct.
All inputs are finite; a program needn't handle non-finite values.
Results may differ from a plain program's by a relative error of at most 0.017.
Values may be sent and summed in bfloat16 or wider, within the bound.
A program may use at most 256 MiB of HBM per device.

v0:
```python
import jax
import jax.numpy as jnp
from jax import lax
from jax.sharding import PartitionSpec as P

SQRT_HALF = 0.7071067811865476
INV_ROOT_TWO_PI = 0.3989422804014327


def gelu_parts(preact):
    normal_cdf = 0.5 * (1.0 + jax.scipy.special.erf(preact * SQRT_HALF))
    return (
        preact * normal_cdf,
        normal_cdf + preact * jnp.exp(-0.5 * preact * preact) * INV_ROOT_TWO_PI,
    )


def per_device(tokens, pattern, blocks, left_factor, right_factor, cotangent):
    tok_rows = tokens.shape[0]
    block_size = blocks.shape[3]
    local_cols = blocks.shape[0]
    slot_count = blocks.shape[1]
    full_tokens = lax.all_gather(tokens, "tensor", axis=1, tiled=True)
    block_count = full_tokens.shape[1] // block_size
    tensor_rank = lax.axis_index("tensor")
    local_pattern = lax.dynamic_slice_in_dim(pattern, tensor_rank * local_cols, local_cols, 0)
    picked = jnp.take(full_tokens.reshape(tok_rows, block_count, block_size), local_pattern, axis=1)
    inputs = picked
    butterfly = jnp.einsum(
        "tjkc,jkcd->tjd",
        inputs,
        lax.all_gather(blocks, "dp", axis=2, tiled=True),
        preferred_element_type=jnp.float32,
    )
    left_rows = lax.all_gather(left_factor, "dp", axis=1, tiled=True)
    whole_left = lax.all_gather(left_rows, "tensor", axis=0, tiled=True)
    rank_acts = jnp.dot(full_tokens, whole_left, preferred_element_type=jnp.float32).astype(
        jnp.bfloat16
    )
    inputs = rank_acts
    rank_part = jnp.dot(
        inputs,
        lax.all_gather(right_factor, "dp", axis=0, tiled=True),
        preferred_element_type=jnp.float32,
    )
    preact = butterfly.reshape(tok_rows, -1) + rank_part
    activated, slope_values = gelu_parts(preact)
    hidden = activated.astype(jnp.bfloat16)
    grad_pre = (cotangent.astype(jnp.float32) * slope_values).astype(jnp.bfloat16)
    rank_terms = lax.dot_general(
        grad_pre,
        lax.all_gather(right_factor, "dp", axis=0, tiled=True),
        (((1,), (1,)), ((), ())),
        preferred_element_type=jnp.float32,
    )
    rank_grad = lax.psum(rank_terms.astype(jnp.bfloat16), "tensor")
    right_term = lax.dot_general(
        rank_acts, grad_pre, (((0,), (0,)), ((), ())), preferred_element_type=jnp.float32
    )
    right_grad = lax.psum_scatter(
        right_term.astype(jnp.bfloat16), "dp", scatter_dimension=0, tiled=True
    ).astype(jnp.float32)
    left_term = lax.dot_general(
        tokens, rank_grad, (((0,), (0,)), ((), ())), preferred_element_type=jnp.float32
    )
    left_grad = lax.psum_scatter(
        left_term.astype(jnp.bfloat16), "dp", scatter_dimension=1, tiled=True
    ).astype(jnp.float32)
    grad_blocks = grad_pre.reshape(tok_rows, local_cols, block_size)
    block_term = jnp.einsum(
        "tjkc,tjd->jkcd", picked, grad_blocks, preferred_element_type=jnp.float32
    )
    block_grad = lax.psum_scatter(
        block_term.astype(jnp.bfloat16), "dp", scatter_dimension=2, tiled=True
    ).astype(jnp.float32)
    spread = jnp.einsum(
        "tjd,jkcd->tjkc",
        grad_blocks,
        lax.all_gather(blocks, "dp", axis=2, tiled=True),
        preferred_element_type=jnp.float32,
    )
    placed = (
        jnp.zeros((tok_rows, block_count, block_size), jnp.float32)
        .at[:, local_pattern.reshape(-1)]
        .add(spread.reshape(tok_rows, local_cols * slot_count, block_size))
    )
    token_part = lax.psum_scatter(
        placed.reshape(tok_rows, -1).astype(jnp.bfloat16), "tensor", scatter_dimension=1, tiled=True
    ).astype(jnp.float32)
    token_grad = token_part + lax.dot_general(
        rank_grad, left_rows, (((1,), (1,)), ((), ())), preferred_element_type=jnp.float32
    )
    return (hidden, token_grad, block_grad, left_grad, right_grad)


def solution(mesh):
    placed = (
        P(("pipe", "dp"), "tensor"),
        P("pipe", None),
        P(("pipe", "tensor"), None, "dp", None),
        P(("pipe", "tensor"), "dp"),
        P(("pipe", "dp"), "tensor"),
        P(("pipe", "dp"), "tensor"),
    )
    return jax.shard_map(
        per_device,
        mesh=mesh,
        in_specs=placed,
        out_specs=(
            P(("pipe", "dp"), "tensor"),
            P(("pipe", "dp"), "tensor"),
            P(("pipe", "tensor"), None, "dp", None),
            P(("pipe", "tensor"), "dp"),
            P(("pipe", "dp"), "tensor"),
        ),
        check_vma=False,
    )
```

profile of v0, /device:TPU:0, one launch (start us, length us, event | category | flops | bytes accessed | tf_op | source)
XLA Modules:
  0.0 936.8 jit_solution(5141369474184893608)
XLA Ops:
  10.6 47.9 %all-gather.10.cloned.1.call-done = bf16[2048,512]{1,0:T(8,128)(2,1)} async-done(((bf16[2048,128]{1,0:T(8,128)(2,1)}), bf16[2048,512]{1,0:T(8,128)(2,1)}) %all-gather.10.cloned.1.call-update) | async-done | bytes 2097168 | tf_op jit(solution)/shard_map/all_gather | solution.py:35
  60.2 45.2 %all-gather.6.cloned.1.call-done = bf16[384,8192]{0,1:T(8,128)(2,1)} async-done(((bf16[384,2048]{0,1:T(8,128)(2,1)}), bf16[384,8192]{0,1:T(8,128)(2,1)}) %all-gather.6.cloned.1.call-update) | async-done | bytes 6291472 | tf_op jit(solution)/shard_map/all_gather | solution.py:23
  105.3 8.6 copy.34
  114.0 13.0 %gather_fusion = bf16[96,384,256]{2,1,0:T(8,128)(2,1)} fusion(bf16[384,32,256]{2,0,1:T(8,128)(2,1)} %copy.34, s32[1024]{0:T(1024)S(1)} %pad_clamp_fusion), kind=kCustom, calls=%fused_computation | custom fusion | bytes 37749120 | tf_op jit(solution)/shard_map/jit(_take)/gather | solution.py:27
  126.9 24.7 %copy.35 = bf16[16,6,384,256]{2,3,1,0:T(8,128)(2,1)} copy(bf16[16,6,384,256]{3,2,1,0:T(8,128)(2,1)} %bitcast.47) | data formatting | bytes 37748736 | tf_op jit(solution)/shard_map/jit(_take)/gather | solution.py:27
  151.6 13.6 %all-gather.12.cloned.1.call-done = bf16[8192,512]{1,0:T(8,128)(2,1)} async-done(((bf16[2048,512]{1,0:T(8,128)(2,1)}), bf16[8192,512]{1,0:T(8,128)(2,1)}) %all-gather.12.cloned.1.call-update) | async-done | bytes 8388624 | tf_op jit(solution)/shard_map/all_gather | solution.py:36
  165.2 8.6 convolution_convert_fusion.3
  173.8 211.0 %all-gather.8.cloned.1.call-done = bf16[16,6,256,256]{3,2,1,0:T(8,128)(2,1)} async-done(((bf16[16,6,64,256]{3,2,1,0:T(8,128)(2,1)}), bf16[16,6,256,256]{3,2,1,0:T(8,128)(2,1)}) %all-gather.8.cloned.1.call-update) | async-done | bytes 12582928 | tf_op jit(solution)/shard_map/all_gather | solution.py:32
  384.9 16.6 %fusion.2 = f32[16,384,256,1]{1,2,3,0:T(8,128)} fusion(bf16[16,6,256,256]{3,2,1,0:T(8,128)(2,1)} %all-gather.8.cloned.1.call-done, bf16[16,6,384,256]{2,3,1,0:T(8,128)(2,1)} %copy.35, pred[16,6]{1,0:T(8,128)(4,1)S(1)} %copy.31), kind=kOutput, calls=%fused_computation.4 | convolution fusion | flops 4841275392 | bytes 37748832 | tf_op jit(solution)/shard_map/tjkc,jkcd->tjd/dot_general | solution.py:29
  401.5 6.6 copy.37
  408.1 57.2 %all-gather.14.cloned.1.call-done = bf16[512,4096]{1,0:T(8,128)(2,1)} async-done(((bf16[128,4096]{1,0:T(8,128)(2,1)}), bf16[512,4096]{1,0:T(8,128)(2,1)}) %all-gather.14.cloned.1.call-update) | async-done | bytes 4194320 | tf_op jit(solution)/shard_map/all_gather | solution.py:43
  465.3 10.5 %fusion.14 = (bf16[384,4096]{1,0:T(8,128)(2,1)S(1)}, bf16[384,4096]{1,0:T(8,128)(2,1)}) fusion(bf16[384,4096]{1,0:T(8,128)(2,1)} %param.11, f32[384,4096]{1,0:T(8,128)} %copy.37, bf16[384,512]{1,0:T(8,128)(2,1)S(1)} %convolution_convert_fusion.3, bf16[512,4096]{1,0:T(8,128)(2,1)} %all-gather.14.cloned.1.call-done), kind=kOutput, calls=%fused_computation.16 | convolution fusion | flops 1632632832 | bytes 20316160 | tf_op jit(solution)/shard_map/dot_general | solution.py:41
  478.7 31.1 %all-reduce.2.cloned.1.call-done = bf16[384,512]{1,0:T(8,128)(2,1)} async-done(((bf16[384,512]{1,0:T(8,128)(2,1)}), bf16[384,512]{1,0:T(8,128)(2,1)}) %all-reduce.2.cloned.1.call-update) | async-done | bytes 393232 | tf_op jit(solution)/shard_map/psum | solution.py:56
  509.8 4.1 fusion.18
  514.0 4.4 convolution_convert_fusion
  522.0 25.2 %fusion.16 = f32[16,384,6,256]{3,1,2,0:T(8,128)} fusion(bf16[16,6,256,256]{3,2,1,0:T(8,128)(2,1)} %all-gather.8.cloned.1.call-done, bf16[384,16,256,1]{2,1,0,3:T(8,128)(2,1)S(1)} %bitcast.50), kind=kOutput, calls=%fused_computation.25 | convolution fusion | flops 4831838208 | bytes 53477376 | tf_op jit(solution)/shard_map/tjd,jkcd->tjkc/dot_general | solution.py:76
  547.2 5.9 broadcast_in_dim.19
  553.1 90.2 %scatter_fusion = f32[384,32,256]{2,0,1:T(8,128)} fusion(f32[384,32,256]{2,0,1:T(8,128)} %broadcast_in_dim.19, s32[96]{0:T(128)S(1)} %fusion.19, f32[96,384,256]{2,1,0:T(8,128)} %bitcast.46), kind=kCustom, calls=%fused_computation.1 | custom fusion | flops 9437184 | bytes 113246592 | tf_op jit(solution)/shard_map/scatter-add | solution.py:85
  643.3 5.4 convert_bitcast_fusion
  654.2 15.2 %fusion.6 = bf16[16,6,256,256]{3,2,1,0:T(8,128)(2,1)} fusion(bf16[16,6,384,256]{2,3,1,0:T(8,128)(2,1)} %copy.35, pred[16,6]{1,0:T(8,128)(4,1)S(1)} %copy.31, bf16[384,16,256,1]{2,1,0,3:T(8,128)(2,1)S(1)} %bitcast.51), kind=kOutput, calls=%fused_computation.10 | convolution fusion | flops 4847566848 | bytes 34603104 | tf_op jit(solution)/shard_map/tjkc,tjd->jkcd/dot_general | solution.py:70
  674.8 35.7 %reduce-scatter.5.cloned.1.call-done = bf16[384,2048]{1,0:T(8,128)(2,1)} async-done(((bf16[384,8192]{1,0:T(8,128)(2,1)}), bf16[384,2048]{1,0:T(8,128)(2,1)}) %reduce-scatter.5.cloned.1.call-update) | async-done | bytes 1572880 | tf_op jit(solution)/shard_map/reduce_scatter | solution.py:87
  710.4 4.1 convert_add_fusion
  714.5 210.0 %reduce-scatter.7.cloned.1.call-done = bf16[16,6,64,256]{3,2,1,0:T(8,128)(2,1)} async-done(((bf16[16,6,256,256]{3,2,1,0:T(8,128)(2,1)}), bf16[16,6,64,256]{3,2,1,0:T(8,128)(2,1)}) %reduce-scatter.7.cloned.1.call-update) | async-done | bytes 3145744 | tf_op jit(solution)/shard_map/reduce_scatter | solution.py:73
  924.5 5.5 convert_element_type.54
  (51 shorter events, 22.1 us)
Async XLA Ops:
  7.2 52.6 %copy-start.5 = (s32[64,6]{0,1:T(8,128)S(1)}, s32[64,6]{0,1:T(8,128)}, u32[]{:S(2)}) copy-start(s32[64,6]{0,1:T(8,128)} %param.7) | copy-start | bytes 4612
  7.2 51.4 %all-gather.10.cloned.1.call-start = ((), (), s32[]{:S(2)}) async-start(), calls=%async_computation.6 | async-start | bytes 2621440 | tf_op jit(solution)/shard_map/all_gather | solution.py:35
  7.9 97.4 %all-gather.6.cloned.1.call-start = ((), (), s32[]{:S(2)}) async-start(), calls=%async_computation.4 | async-start | bytes 7864320 | tf_op jit(solution)/shard_map/all_gather | solution.py:23
  10.6 154.6 %all-gather.12.cloned.1.call-start = ((), (), s32[]{:S(2)}) async-start(), calls=%async_computation.7 | async-start | bytes 10485760 | tf_op jit(solution)/shard_map/all_gather | solution.py:36
  58.6 326.3 %all-gather.8.cloned.1.call-start = ((), (), s32[]{:S(2)}) async-start(), calls=%async_computation.5 | async-start | bytes 15728640 | tf_op jit(solution)/shard_map/all_gather | solution.py:32
  59.1 406.1 %all-gather.14.cloned.1.call-start = ((), (), s32[]{:S(2)}) async-start(), calls=%async_computation.8 | async-start | bytes 5242880 | tf_op jit(solution)/shard_map/all_gather | solution.py:43
  59.7 450.0 %all-reduce.2.cloned.1.call-start = ((), (), s32[]{:S(2)}) async-start(), calls=%async_computation.10 | async-start | bytes 786432 | tf_op jit(solution)/shard_map/psum | solution.py:56
  465.3 10.5 %copy-start.6 = (bf16[512,4096]{1,0:T(8,128)(2,1)S(1)}, bf16[512,4096]{1,0:T(8,128)(2,1)}, u32[]{:S(2)}) copy-start(bf16[512,4096]{1,0:T(8,128)(2,1)} %all-gather.14.cloned.1.call-done) | copy-start | bytes 12582916
  475.8 38.2 %copy-start.2 = (bf16[384,4096]{1,0:T(8,128)(2,1)}, bf16[384,4096]{1,0:T(8,128)(2,1)S(1)}, u32[]{:S(2)}) copy-start(bf16[384,4096]{1,0:T(8,128)(2,1)S(1)} %get-tuple-element.22) | copy-start | bytes 9437188
  478.5 191.0 %reduce-scatter.9.cloned.1.call-start = ((), (), s32[]{:S(2)}) async-start(), calls=%async_computation.12 | async-start | bytes 2621440 | tf_op jit(solution)/shard_map/reduce_scatter | solution.py:66
  513.9 157.9 %reduce-scatter.11.cloned.1.call-start = ((), (), s32[]{:S(2)}) async-start(), calls=%async_computation.13 | async-start | bytes 5242880 | tf_op jit(solution)/shard_map/reduce_scatter | solution.py:60
  518.5 192.0 %reduce-scatter.5.cloned.1.call-start = ((), (), s32[]{:S(2)}) async-start(), calls=%async_computation.9 | async-start | bytes 7864320 | tf_op jit(solution)/shard_map/reduce_scatter | solution.py:87
  522.0 25.2 %copy-start = (bf16[48,8,16,256]{3,2,1,0:T(8,128)(2,1)}, bf16[48,8,16,256]{3,2,1,0:T(8,128)(2,1)S(1)}, u32[]{:S(2)}) copy-start(bf16[48,8,16,256]{3,2,1,0:T(8,128)(2,1)S(1)} %copy.52) | copy-start | bytes 9437188
  652.3 1.9 copy-start.1
  652.3 272.2 %reduce-scatter.7.cloned.1.call-start = ((), (), s32[]{:S(2)}) async-start(), calls=%async_computation.11 | async-start | bytes 15728640 | tf_op jit(solution)/shard_map/reduce_scatter | solution.py:73
  669.4 41.0 %copy-start.3 = (bf16[2048,512]{1,0:T(8,128)(2,1)S(1)}, bf16[2048,512]{1,0:T(8,128)(2,1)}, u32[]{:S(2)}) copy-start(bf16[2048,512]{1,0:T(8,128)(2,1)} %all-gather.10.cloned.1.call-done) | copy-start | bytes 6291460
  669.4 41.0 %copy-start.4 = (bf16[384,512]{1,0:T(8,128)(2,1)S(1)}, bf16[384,512]{1,0:T(8,128)(2,1)}, u32[]{:S(2)}) copy-start(bf16[384,512]{1,0:T(8,128)(2,1)} %all-reduce.2.cloned.1.call-done) | copy-start | bytes 1179652
Sparse Core Ops, SparseCore 0:
  9.6 48.9 all-gather.9
  60.7 44.5 all-gather.5
  106.9 58.2 all-gather.11
  166.6 218.2 all-gather.7
  386.3 78.9 all-gather.13
  478.6 31.1 all-reduce.1
  514.0 43.8 reduce-scatter.8
  560.2 76.0 reduce-scatter.10
  652.4 57.9 reduce-scatter.4
  712.6 211.8 reduce-scatter.6
where the time goes:
time: 939 us; the launch traced here: 937 us
  waiting for transfers between devices  654 us (70%)
  other arithmetic  104 us (11%)
  matrix products  91.5 us (10%)
  local copies, waits for them, and re-layouts  72.6 us (8%)
  between operations  14.3 us (2%)
    all_gather x1, waiting for transfers between devices, per_device(): lax.all_gather(blocks, 'dp', axis=2, tiled=True)  211 us
    reduce_scatter x1, waiting for transfers between devices, per_device(): lax.psum_scatter(block_term.astype(jnp.bfloat16), 'dp', scatter_dimension...  210 us
    scatter-add x1, other arithmetic, per_device(): placed = jnp.zeros((tok_rows, block_count, block_size), jnp.float32).at[:...  90.2 us
    all_gather x1, waiting for transfers between devices, per_device(): lax.all_gather(right_factor, 'dp', axis=0, tiled=True)  57.2 us
    all_gather x1, waiting for transfers between devices, per_device(): left_rows = lax.all_gather(left_factor, 'dp', axis=1, tiled=True)  47.9 us
    all_gather x1, waiting for transfers between devices, per_device(): full_tokens = lax.all_gather(tokens, 'tensor', axis=1, tiled=True)  45.2 us
    gather x2, local copies, waits for them, and re-layouts, per_device(): jnp.take(full_tokens.reshape(tok_rows, block_count, block_size), local_pa...  37.6 us
    reduce_scatter x1, waiting for transfers between devices, per_device(): lax.psum_scatter(placed.reshape(tok_rows, -1).astype(jnp.bfloat16), 'tens...  35.7 us
  transfers between devices with their start and end apart: 10, of which 8 were waited for; matrix products, arithmetic and copies ran while one was open for 26% of the time, Pallas kernels for 0%

commit v1 on v0

--- a/solution.py
+++ b/solution.py
@@ -26,11 +26,26 @@
     local_pattern = lax.dynamic_slice_in_dim(pattern, tensor_rank * local_cols, local_cols, 0)
     picked = jnp.take(full_tokens.reshape(tok_rows, block_count, block_size), local_pattern, axis=1)
     inputs = picked
-    butterfly = jnp.einsum(
-        "tjkc,jkcd->tjd",
-        inputs,
-        lax.all_gather(blocks, "dp", axis=2, tiled=True),
-        preferred_element_type=jnp.float32,
+
+    def view_words_on(page, local_block):
+        back, carry_in, earlier = (lax.axis_size("dp"), lax.axis_index("dp"), page.shape[2])
+        front, carry = (page, None)
+        lanes = [(num, (num + 1) % back) for num in range(back)]
+        for dev in range(back):
+            met_up = lax.ppermute(front, axis_name="dp", perm=lanes) if dev < back - 1 else None
+            now = local_block(front, (carry_in - dev) % back * earlier)
+            carry = now if carry is None else carry + now
+            front = met_up
+        return carry
+
+    butterfly = view_words_on(
+        blocks,
+        lambda own_block, offset: jnp.einsum(
+            "tjkc,jkcd->tjd",
+            lax.dynamic_slice_in_dim(inputs, offset, own_block.shape[2], axis=3),
+            own_block,
+            preferred_element_type=jnp.float32,
+        ),
     )
     left_rows = lax.all_gather(left_factor, "dp", axis=1, tiled=True)
     whole_left = lax.all_gather(left_rows, "tensor", axis=0, tiled=True)

time: 939 us -> 1040 us (1.11)
  waiting for transfers between devices: 654 us -> 729 us
  other arithmetic: 104 us -> 118 us
    ppermute x0 -> x3, waiting for transfers between devices: none -> 190 us  [view_words_on(): lax.ppermute(front, axis_name='dp', perm=lanes)]
    all_gather x1, waiting for transfers between devices: 57.2 us -> 0.02 us  [per_device(): lax.all_gather(right_factor, 'dp', axis=0, tiled=True)]
    all_gather x1, waiting for transfers between devices: 45.2 us -> 0.01 us  [per_device(): full_tokens = lax.all_gather(tokens, 'tensor', axis=1, tiled=True)]
    dot_general x1 -> x4, matrix products: 16.6 us -> 34.7 us  [per_device(): jnp.einsum('tjkc,jkcd->tjd', lax.dynamic_slice_in_dim(inputs, offset, own...]
    all_gather x1, waiting for transfers between devices: 13.6 us -> 0.01 us  [per_device(): whole_left = lax.all_gather(left_rows, 'tensor', axis=0, tiled=True)]
  transfers between devices with their start and end apart: 10 -> 13, of which waited for: 8 -> 8; matrix products, arithmetic and copies ran while one was open for 26% -> 26% of each run, Pallas kernels for 0% -> 0%
where the time goes in v1:
time: 1040 us
  waiting for transfers between devices  729 us (70%)
  other arithmetic  118 us (11%)
  matrix products  96.7 us (9%)
  local copies, waits for them, and re-layouts  72.3 us (7%)
  between operations  14.4 us (1%)
    reduce_scatter x1, waiting for transfers between devices, per_device(): lax.psum_scatter(block_term.astype(jnp.bfloat16), 'dp', scatter_dimension...  210 us
    all_gather x1, waiting for transfers between devices, per_device(): lax.all_gather(blocks, 'dp', axis=2, tiled=True)  208 us
    ppermute x3, waiting for transfers between devices, view_words_on(): lax.ppermute(front, axis_name='dp', perm=lanes)  190 us
    scatter-add x1, other arithmetic, per_device(): placed = jnp.zeros((tok_rows, block_count, block_size), jnp.float32).at[:...  90.1 us
    all_gather x1, waiting for transfers between devices, per_device(): left_rows = lax.all_gather(left_factor, 'dp', axis=1, tiled=True)  47.8 us
    reduce_scatter x1, waiting for transfers between devices, per_device(): lax.psum_scatter(placed.reshape(tok_rows, -1).astype(jnp.bfloat16), 'tens...  39.3 us
    gather x2, local copies, waits for them, and re-layouts, per_device(): jnp.take(full_tokens.reshape(tok_rows, block_count, block_size), local_pa...  36.6 us
    dot_general x4, matrix products, per_device(): jnp.einsum('tjkc,jkcd->tjd', lax.dynamic_slice_in_dim(inputs, offset, own...  34.7 us
  transfers between devices with their start and end apart: 13, of which 8 were waited for; matrix products, arithmetic and copies ran while one was open for 26% of the time, Pallas kernels for 0%

profile of v1, /device:TPU:0, one launch (start us, length us, event | category | flops | bytes accessed | tf_op | source)
XLA Modules:
  0.0 1040.4 jit_solution(16582622014454873347)
XLA Ops:
  10.8 47.8 %all-gather.8.cloned.1.call-done = bf16[2048,512]{1,0:T(8,128)(2,1)} async-done(((bf16[2048,128]{1,0:T(8,128)(2,1)}), bf16[2048,512]{1,0:T(8,128)(2,1)}) %all-gather.8.cloned.1.call-update) | async-done | bytes 2097168 | tf_op jit(solution)/shard_map/all_gather | solution.py:50
  58.9 70.9 %collective-permute-done = bf16[16,6,64,256]{3,2,1,0:T(8,128)(2,1)} collective-permute-done((bf16[16,6,64,256]{3,2,1,0:T(8,128)(2,1)S(1)}, bf16[16,6,64,256]{3,2,1,0:T(8,128)(2,1)}, u32[]{:S(2)}, u32[]{:S(2)}) %collective-permute-start) | collective-permute-done | bytes 3145760 | tf_op jit(solution)/shard_map/ppermute | solution.py:35
  130.3 93.0 %collective-permute-done.1 = bf16[16,6,64,256]{3,2,1,0:T(8,128)(2,1)} collective-permute-done((bf16[16,6,64,256]{3,2,1,0:T(8,128)(2,1)}, bf16[16,6,64,256]{3,2,1,0:T(8,128)(2,1)}, u32[]{:S(2)}, u32[]{:S(2)}) %collective-permute-start.1) | collective-permute-done | bytes 3145760 | tf_op jit(solution)/shard_map/ppermute | solution.py:35
  223.4 9.0 collective-permute-start.2
  232.3 8.6 copy.31
  241.0 11.9 %gather_fusion = bf16[96,384,256]{2,1,0:T(8,128)(2,1)} fusion(bf16[384,32,256]{2,0,1:T(8,128)(2,1)} %copy.31, s32[1024]{0:T(1024)S(1)} %pad_clamp_fusion), kind=kCustom, calls=%fused_computation | custom fusion | bytes 37749120 | tf_op jit(solution)/shard_map/jit(_take)/gather | solution.py:27
  252.9 24.6 %copy.32 = bf16[96,384,256]{1,2,0:T(8,128)(2,1)} copy(bf16[96,384,256]{2,1,0:T(8,128)(2,1)} %gather_fusion) | data formatting | bytes 37748736 | tf_op jit(solution)/shard_map/jit(_take)/gather | solution.py:27
  277.6 10.3 broadcast_select_fusion
  293.2 9.1 fusion.13
  302.3 6.7 fusion.15
  309.0 26.1 %collective-permute-done.2 = bf16[16,6,64,256]{3,2,1,0:T(8,128)(2,1)} collective-permute-done((bf16[16,6,64,256]{3,2,1,0:T(8,128)(2,1)}, bf16[16,6,64,256]{3,2,1,0:T(8,128)(2,1)}, u32[]{:S(2)}, u32[]{:S(2)}) %collective-permute-start.2) | collective-permute-done | bytes 3145760 | tf_op jit(solution)/shard_map/ppermute | solution.py:35
  335.1 13.6 %bitcast_add_fusion = f32[16,384,256]{1,2,0:T(8,128)} fusion(f32[16,384,256,1]{1,2,3,0:T(8,128)} %fusion.13, f32[16,384,256,1]{1,2,3,0:T(8,128)} %fusion.15, f32[16,384,256,1]{1,2,3,0:T(8,128)} %fusion.17, bf16[16,6,64,256]{3,2,1,0:T(8,128)(2,1)} %collective-permute-done.2, bf16[16,6,384,256]{2,3,1,0:T(8,128)(2,1)} %copy-done, s32[]{:T(128)S(6)} %select_n.63), kind=kOutput, calls=%fused_computation.13 | convolution fusion | flops 1212678144 | bytes 33030148 | tf_op jit(solution)/shard_map/tjkc,jkcd->tjd/dot_general | solution.py:43
  348.8 6.6 copy.33
  355.4 8.6 convolution_convert_fusion.3
  376.5 32.1 %all-reduce.2.cloned.1.call-done = bf16[384,512]{1,0:T(8,128)(2,1)} async-done(((bf16[384,512]{1,0:T(8,128)(2,1)}), bf16[384,512]{1,0:T(8,128)(2,1)}) %all-reduce.2.cloned.1.call-update) | async-done | bytes 393232 | tf_op jit(solution)/shard_map/psum | solution.py:71
  420.3 208.2 %all-gather.14.cloned.1.call-done = bf16[16,6,256,256]{3,2,1,0:T(8,128)(2,1)} async-done(((bf16[16,6,64,256]{3,2,1,0:T(8,128)(2,1)}), bf16[16,6,256,256]{3,2,1,0:T(8,128)(2,1)}) %all-gather.14.cloned.1.call-update) | async-done | bytes 12582928 | tf_op jit(solution)/shard_map/all_gather | solution.py:94
  628.4 20.3 %fusion.24 = f32[16,384,6,256]{3,1,2,0:T(8,128)} fusion(bf16[16,6,256,256]{3,2,1,0:T(8,128)(2,1)} %all-gather.14.cloned.1.call-done, bf16[384,16,256,1]{2,1,0,3:T(8,128)(2,1)} %bitcast.80), kind=kOutput, calls=%fused_computation.35 | convolution fusion | flops 4831838208 | bytes 53477376 | tf_op jit(solution)/shard_map/tjd,jkcd->tjkc/dot_general | solution.py:91
  648.7 6.0 broadcast_in_dim.19
  654.7 90.1 %scatter_fusion = f32[384,32,256]{2,0,1:T(8,128)} fusion(f32[384,32,256]{2,0,1:T(8,128)} %broadcast_in_dim.19, s32[96]{0:T(128)S(1)} %fusion.33, f32[96,384,256]{2,1,0:T(8,128)} %bitcast.74), kind=kCustom, calls=%fused_computation.1 | custom fusion | flops 9437184 | bytes 113246592 | tf_op jit(solution)/shard_map/scatter-add | solution.py:100
  744.8 5.5 convert_bitcast_fusion
  755.7 13.8 %fusion.2 = bf16[16,6,256,256]{3,2,1,0:T(8,128)(2,1)} fusion(bf16[16,6,384,256]{2,3,1,0:T(8,128)(2,1)} %copy-done, bf16[384,16,256,1]{2,1,0,3:T(8,128)(2,1)S(1)} %bitcast.81), kind=kOutput, calls=%fused_computation.6 | convolution fusion | flops 4838129664 | bytes 34603008 | tf_op jit(solution)/shard_map/tjkc,tjd->jkcd/dot_general | solution.py:85
  774.7 39.3 %reduce-scatter.5.cloned.1.call-done = bf16[384,2048]{1,0:T(8,128)(2,1)} async-done(((bf16[384,8192]{1,0:T(8,128)(2,1)}), bf16[384,2048]{1,0:T(8,128)(2,1)}) %reduce-scatter.5.cloned.1.call-update) | async-done | bytes 1572880 | tf_op jit(solution)/shard_map/reduce_scatter | solution.py:102
  818.1 210.0 %reduce-scatter.7.cloned.1.call-done = bf16[16,6,64,256]{3,2,1,0:T(8,128)(2,1)} async-done(((bf16[16,6,256,256]{3,2,1,0:T(8,128)(2,1)}), bf16[16,6,64,256]{3,2,1,0:T(8,128)(2,1)}) %reduce-scatter.7.cloned.1.call-update) | async-done | bytes 3145744 | tf_op jit(solution)/shard_map/reduce_scatter | solution.py:88
  1028.1 5.5 convert_element_type.54
  (66 shorter events, 48.2 us)
Async XLA Ops:
  7.2 51.5 %copy-start.3 = (bf16[16,6,64,256]{3,2,1,0:T(8,128)(2,1)S(1)}, bf16[16,6,64,256]{3,2,1,0:T(8,128)(2,1)}, u32[]{:S(2)}) copy-start(bf16[16,6,64,256]{3,2,1,0:T(8,128)(2,1)} %param.8) | copy-start | bytes 9437188
  7.2 122.7 %copy-start.8 = (s32[64,6]{0,1:T(8,128)S(1)}, s32[64,6]{0,1:T(8,128)}, u32[]{:S(2)}) copy-start(s32[64,6]{0,1:T(8,128)} %param.7) | copy-start | bytes 4612
  7.2 51.4 %all-gather.8.cloned.1.call-start = ((), (), s32[]{:S(2)}) async-start(), calls=%async_computation.5 | async-start | bytes 2621440 | tf_op jit(solution)/shard_map/all_gather | solution.py:50
  7.9 224.4 %all-gather.6.cloned.1.call-start = ((), (), s32[]{:S(2)}) async-start(), calls=%async_computation.4 | async-start | bytes 7864320 | tf_op jit(solution)/shard_map/all_gather | solution.py:23
  10.7 344.7 %all-gather.10.cloned.1.call-start = ((), (), s32[]{:S(2)}) async-start(), calls=%async_computation.6 | async-start | bytes 10485760 | tf_op jit(solution)/shard_map/all_gather | solution.py:51
  58.6 305.5 %all-gather.12.cloned.1.call-start = ((), (), s32[]{:S(2)}) async-start(), calls=%async_computation.7 | async-start | bytes 5242880 | tf_op jit(solution)/shard_map/all_gather | solution.py:58
  58.6 71.1 %collective-permute-start = (bf16[16,6,64,256]{3,2,1,0:T(8,128)(2,1)S(1)}, bf16[16,6,64,256]{3,2,1,0:T(8,128)(2,1)}, u32[]{:S(2)}, u32[]{:S(2)}) collective-permute-start(bf16[16,6,64,256]{3,2,1,0:T(8,128)(2,1)S(1)} %copy-done.3), channel_id=1, source_target_pairs={{0,4},{4,8},{8,12},{12,0},{1,5},{5,9},{9,13},{13,1},{2,6},{6,10},{... | collective-permute-start | bytes 9437192 | tf_op jit(solution)/shard_map/ppermute | solution.py:35
  129.8 93.6 %collective-permute-start.1 = (bf16[16,6,64,256]{3,2,1,0:T(8,128)(2,1)}, bf16[16,6,64,256]{3,2,1,0:T(8,128)(2,1)}, u32[]{:S(2)}, u32[]{:S(2)}) collective-permute-start(bf16[16,6,64,256]{3,2,1,0:T(8,128)(2,1)} %collective-permute-done), channel_id=1, source_target_pairs={{0,4},{4,8},{8,12},{12,0},{1,5},{5,9},{9,13},{13,1},{2,6},{6,10},{... | collective-permute-start | bytes 9437192 | tf_op jit(solution)/shard_map/ppermute | solution.py:35
  129.8 278.8 %all-reduce.2.cloned.1.call-start = ((), (), s32[]{:S(2)}) async-start(), calls=%async_computation.10 | async-start | bytes 786432 | tf_op jit(solution)/shard_map/psum | solution.py:71
  223.4 111.7 %collective-permute-start.2 = (bf16[16,6,64,256]{3,2,1,0:T(8,128)(2,1)}, bf16[16,6,64,256]{3,2,1,0:T(8,128)(2,1)}, u32[]{:S(2)}, u32[]{:S(2)}) collective-permute-start(bf16[16,6,64,256]{3,2,1,0:T(8,128)(2,1)} %collective-permute-done.1), channel_id=1, source_target_pairs={{0,4},{4,8},{8,12},{12,0},{1,5},{5,9},{9,13},{13,1},{2,6},{6,10},{... | collective-permute-start | bytes 9437192 | tf_op jit(solution)/shard_map/ppermute | solution.py:35
  287.9 14.4 %copy-start = (bf16[16,6,384,256]{2,3,1,0:T(8,128)(2,1)}, bf16[16,6,384,256]{2,3,1,0:T(8,128)(2,1)S(1)}, u32[]{:S(2)}) copy-start(bf16[16,6,384,256]{2,3,1,0:T(8,128)(2,1)S(1)} %broadcast_select_fusion) | copy-start | bytes 56623108
  364.1 4.2 copy-start.1
  364.1 5.0 copy-start.6
  369.0 4.2 copy-start.5
  375.8 252.6 %all-gather.14.cloned.1.call-start = ((), (), s32[]{:S(2)}) async-start(), calls=%async_computation.8 | async-start | bytes 15728640 | tf_op jit(solution)/shard_map/all_gather | solution.py:94
  376.4 393.1 %reduce-scatter.9.cloned.1.call-start = ((), (), s32[]{:S(2)}) async-start(), calls=%async_computation.12 | async-start | bytes 2621440 | tf_op jit(solution)/shard_map/reduce_scatter | solution.py:81
  412.8 359.2 %reduce-scatter.11.cloned.1.call-start = ((), (), s32[]{:S(2)}) async-start(), calls=%async_computation.13 | async-start | bytes 5242880 | tf_op jit(solution)/shard_map/reduce_scatter | solution.py:75
  417.2 396.8 %reduce-scatter.5.cloned.1.call-start = ((), (), s32[]{:S(2)}) async-start(), calls=%async_computation.9 | async-start | bytes 7864320 | tf_op jit(solution)/shard_map/reduce_scatter | solution.py:102
  753.8 1.9 copy-start.2
  753.8 274.3 %reduce-scatter.7.cloned.1.call-start = ((), (), s32[]{:S(2)}) async-start(), calls=%async_computation.11 | async-start | bytes 15728640 | tf_op jit(solution)/shard_map/reduce_scatter | solution.py:88
  769.5 44.5 %copy-start.4 = (bf16[2048,512]{1,0:T(8,128)(2,1)S(1)}, bf16[2048,512]{1,0:T(8,128)(2,1)}, u32[]{:S(2)}) copy-start(bf16[2048,512]{1,0:T(8,128)(2,1)} %all-gather.8.cloned.1.call-done) | copy-start | bytes 6291460
  769.5 44.5 %copy-start.7 = (bf16[384,512]{1,0:T(8,128)(2,1)S(1)}, bf16[384,512]{1,0:T(8,128)(2,1)}, u32[]{:S(2)}) copy-start(bf16[384,512]{1,0:T(8,128)(2,1)} %all-reduce.2.cloned.1.call-done) | copy-start | bytes 1179652
Sparse Core Ops, SparseCore 0:
  9.6 48.9 all-gather.7
  60.7 44.5 all-gather.5
  106.9 58.2 all-gather.9
  166.6 135.4 all-gather.11
  376.0 32.6 all-reduce.1
  410.1 218.2 all-gather.13
  631.4 41.9 reduce-scatter.8
  675.7 76.0 reduce-scatter.10
  755.1 58.8 reduce-scatter.4
  816.2 211.8 reduce-scatter.6
